TPU v7x, 32 devices: a whole 2x2x4 slice. The times are simulated.
32 devices in a mesh: dp: 16 (over z, x, core), seq: 2 (over y).
Axes of the slice: x: 2, y: 2, z: 4, core: 2. Of those that a mesh axis runs over, the one named last changes fastest.
Arguments:
- inputs: float32 [16, 512, 1280], P('dp', 'seq'), may hold values from -6 to 6
- cotangent: float32 [16, 512, 1280], P('dp', 'seq'), may hold values from -6 to 6
- starts: int32 [16, 4], P('dp'), may hold values from 0 to 511, as said below
- weights: float32 [1280, 7680], P('dp')
- weight_m: float32 [1280, 7680], P('dp')
- weight_v: float32 [1280, 7680], P('dp')
- gains: float32 [2, 1280], P(None, 'dp'), may hold values from 0.5 to 1.5
- gain_m: float32 [2, 1280], P(None, 'dp'), may hold values from -512 to 512
- gain_v: float32 [2, 1280], P(None, 'dp'), may hold values from 8192 to 32768
- qscale: float32 [80], replicated, may hold values from -3 to 3
- qscale_m: float32 [80], replicated, may hold values from -512 to 512
- qscale_v: float32 [80], replicated, may hold values from 8192 to 32768
Outputs:
- outputs: float32 [16, 512, 1280], P('dp', 'seq')
- input_grad: float32 [16, 512, 1280], P('dp', 'seq')
- weights_new: float32 [1280, 7680], P('dp')
- weight_m_new: float32 [1280, 7680], P('dp')
- weight_v_new: float32 [1280, 7680], P('dp')
- weights_low: bfloat16 [1280, 7680], P('dp')
- gains_new: float32 [2, 1280], P(None, 'dp')
- gain_m_new: float32 [2, 1280], P(None, 'dp')
- gain_v_new: float32 [2, 1280], P(None, 'dp')
- qscale_new: float32 [80], replicated
- qscale_m_new: float32 [80], replicated
- qscale_v_new: float32 [80], replicated
Inputs may be any that keep to these rules, and one draw needn't show every extreme that they name: `starts`: each row is 4 increasing start positions, the first 0; one document of each stream begins within the first 256 positions and ends within the last 256.
All inputs are finite; a program needn't handle non-finite values.
Results may differ from a plain program's by a relative error of at most 0.022.
The roundings to bfloat16 on the way count: a program that leaves them out, or rounds other values in their place, can miss the bound.
Values may be sent and summed in bfloat16 or wider, within the bound.
A program may use at most 192 MiB of HBM per device.

v0:
```python
import math

import jax
import jax.numpy as jnp
from jax import lax
from jax.sharding import PartitionSpec as P

HEADS = 16
STEP = 10


EPS = 1e-06
QUERY_BASE = 1.442695
BETA_ONE = 0.5
BETA_TWO = 0.5
ADAM_EPS = 1e-08
RATE_MATRIX = 0.02
RATE_GAIN = 0.3
DECAY = 0.1
NEG = -1e30


def norm_forward(values, gain):
    inverse = lax.rsqrt(jnp.mean(values * values, axis=-1, keepdims=True) + EPS)
    normed = values * inverse
    return (normed, inverse, (normed * gain).astype(jnp.bfloat16))


def norm_backward(grad, normed, inverse, gain):
    gain_grad = jnp.sum(grad * normed, axis=0)
    scaled = grad * gain
    return (
        inverse * (scaled - normed * jnp.mean(scaled * normed, axis=-1, keepdims=True)),
        gain_grad,
    )


def adamw(param, grad, first, second, rate):
    first_new = BETA_ONE * first + (1.0 - BETA_ONE) * grad
    second_new = BETA_TWO * second + (1.0 - BETA_TWO) * grad * grad
    first_hat = first_new / (1.0 - BETA_ONE**STEP)
    second_hat = second_new / (1.0 - BETA_TWO**STEP)
    param_new = param - rate * (first_hat / (jnp.sqrt(second_hat) + ADAM_EPS) + DECAY * param)
    return (param_new, first_new, second_new)


def on_device(
    inputs,
    cotangent,
    starts,
    weights,
    weight_m,
    weight_v,
    gains,
    gain_m,
    gain_v,
    qscale,
    qscale_m,
    qscale_v,
):
    full_w, full_g = (
        lax.all_gather(weights.astype(jnp.bfloat16), "dp", axis=0, tiled=True),
        lax.all_gather(gains.astype(jnp.bfloat16), "dp", axis=1, tiled=True),
    )
    width = full_w.shape[0]
    head_dim = width // HEADS
    w_qkv = full_w[:, : 3 * width]
    w_out = full_w[:, 3 * width : 4 * width]
    w_up = full_w[:, 4 * width : 5 * width]
    w_down = full_w[:, 5 * width :]
    gain_one = full_g[0].astype(jnp.float32)
    gain_two = full_g[1].astype(jnp.float32)
    resid = inputs[0]
    count = resid.shape[0]
    groups = lax.axis_size("seq")
    length = count * groups
    local_width = width // groups
    local_heads = local_width // head_dim
    block = min(512, length)
    blocks = length // block
    normed_one, inverse_one, hidden_one = norm_forward(resid, gain_one)
    projected = jnp.dot(hidden_one, w_qkv, preferred_element_type=jnp.float32).reshape(
        count, 3, width
    )
    base_scale = QUERY_BASE / math.sqrt(head_dim)
    tiled = jnp.tile(base_scale * jax.nn.softplus(qscale), HEADS)
    factor = jnp.stack([tiled, jnp.ones_like(tiled), jnp.ones_like(tiled)])
    outgoing = (projected * factor[None]).astype(jnp.bfloat16)
    arrived = lax.all_to_all(outgoing, "seq", split_axis=2, concat_axis=0, tiled=True)
    queries = arrived[:, 0].reshape(length, local_heads, head_dim)
    keys = arrived[:, 1].reshape(length, local_heads, head_dim)
    values = arrived[:, 2].reshape(length, local_heads, head_dim)
    positions = jnp.arange(length, dtype=jnp.int32)
    segment = jnp.sum((positions[:, None] >= starts[0][None, :]).astype(jnp.int32), axis=1) - 1

    def masked_scores(start):
        query_block = lax.dynamic_slice_in_dim(queries, start, block, 0)
        raw = jnp.einsum("qhd,khd->hqk", query_block, keys, preferred_element_type=jnp.float32)
        rows = start + jnp.arange(block, dtype=jnp.int32)
        row_seg = lax.dynamic_slice_in_dim(segment, start, block, 0)
        allowed = (positions[None, :] <= rows[:, None]) & (segment[None, :] == row_seg[:, None])
        return (query_block, jnp.where(allowed[None], raw, NEG))

    def forward_block(index):
        query_block, masked = masked_scores(index * block)
        top = jnp.max(masked, axis=-1, keepdims=True)
        expo = jnp.exp(masked - top)
        total = jnp.sum(expo, axis=-1, keepdims=True)
        probs = (expo / total).astype(jnp.bfloat16)
        attended = jnp.einsum("hqk,khd->qhd", probs, values, preferred_element_type=jnp.float32)
        return (attended.astype(jnp.bfloat16), (top + jnp.log(total))[..., 0])

    head_out, log_totals = lax.map(forward_block, jnp.arange(blocks, dtype=jnp.int32))
    head_out = head_out.reshape(length, local_width)
    attn_rows = lax.all_to_all(head_out, "seq", split_axis=0, concat_axis=1, tiled=True)
    mixed = resid + jnp.dot(attn_rows, w_out, preferred_element_type=jnp.float32)
    normed_two, inverse_two, hidden_two = norm_forward(mixed, gain_two)
    gate = jnp.dot(hidden_two, w_up, preferred_element_type=jnp.float32)
    sigma = jax.nn.sigmoid(gate)
    activ = (gate * sigma).astype(jnp.bfloat16)
    outputs = mixed + jnp.dot(activ, w_down, preferred_element_type=jnp.float32)
    grad_top = cotangent[0]
    grad_low = grad_top.astype(jnp.bfloat16)
    grad_activ = jnp.dot(grad_low, w_down.T, preferred_element_type=jnp.float32)
    grad_gate = (grad_activ * sigma * (1.0 + gate * (1.0 - sigma))).astype(jnp.bfloat16)
    grad_down = jnp.dot(activ.T, grad_low, preferred_element_type=jnp.float32)
    grad_up = jnp.dot(hidden_two.T, grad_gate, preferred_element_type=jnp.float32)
    grad_hidden_two = jnp.dot(grad_gate, w_up.T, preferred_element_type=jnp.float32)
    grad_norm_two, gain_grad_two = norm_backward(grad_hidden_two, normed_two, inverse_two, gain_two)
    grad_mixed = grad_top + grad_norm_two
    mixed_low = grad_mixed.astype(jnp.bfloat16)
    grad_out = jnp.dot(attn_rows.T, mixed_low, preferred_element_type=jnp.float32)
    grad_attn = jnp.dot(mixed_low, w_out.T, preferred_element_type=jnp.float32).astype(jnp.bfloat16)
    grad_heads = lax.all_to_all(grad_attn, "seq", split_axis=1, concat_axis=0, tiled=True).reshape(
        length, local_heads, head_dim
    )

    def backward_block(carry, index):
        key_sum, value_sum = carry
        start = index * block
        query_block, masked = masked_scores(start)
        grad_block = lax.dynamic_slice_in_dim(grad_heads, start, block, 0)
        lse_block = log_totals[index]
        probs = jnp.exp(masked - lse_block[:, :, None])
        value_sum = value_sum + jnp.einsum(
            "hqk,qhd->khd",
            probs.astype(jnp.bfloat16),
            grad_block,
            preferred_element_type=jnp.float32,
        )
        grad_probs = jnp.einsum(
            "qhd,khd->hqk", grad_block, values, preferred_element_type=jnp.float32
        )
        grad_scores = probs * (grad_probs - jnp.sum(probs * grad_probs, axis=-1, keepdims=True))
        scores_low = grad_scores.astype(jnp.bfloat16)
        grad_query = jnp.einsum(
            "hqk,khd->qhd", scores_low, keys, preferred_element_type=jnp.float32
        )
        key_sum = key_sum + jnp.einsum(
            "hqk,qhd->khd", scores_low, query_block, preferred_element_type=jnp.float32
        )
        return ((key_sum, value_sum), grad_query)

    empty = jnp.zeros((length, local_heads, head_dim), jnp.float32)
    (key_grad, value_grad), query_grad = lax.scan(
        backward_block, (empty, empty), jnp.arange(blocks, dtype=jnp.int32)
    )
    stacked = jnp.stack(
        [
            query_grad.reshape(length, local_width),
            key_grad.reshape(length, local_width),
            value_grad.reshape(length, local_width),
        ],
        axis=1,
    ).astype(jnp.bfloat16)
    returned = lax.all_to_all(stacked, "seq", split_axis=0, concat_axis=2, tiled=True)
    scaled_grad = returned[:, 0].astype(jnp.float32)
    scale_part = jnp.sum(scaled_grad * projected[:, 0], axis=0).reshape(HEADS, head_dim).sum(axis=0)
    query_low = (scaled_grad * tiled[None]).astype(jnp.bfloat16)
    grad_qkv_rows = jnp.concatenate([query_low[:, None], returned[:, 1:]], axis=1).reshape(
        count, 3 * width
    )
    grad_qkv = jnp.dot(hidden_one.T, grad_qkv_rows, preferred_element_type=jnp.float32)
    grad_hidden_one = jnp.dot(grad_qkv_rows, w_qkv.T, preferred_element_type=jnp.float32)
    grad_norm_one, gain_grad_one = norm_backward(grad_hidden_one, normed_one, inverse_one, gain_one)
    input_grad = grad_mixed + grad_norm_one
    all_grads = jnp.concatenate([grad_qkv, grad_out, grad_up, grad_down], axis=1)
    gain_grads = jnp.stack([gain_grad_one, gain_grad_two])
    owned_w, owned_g = (
        lax.psum_scatter(
            all_grads.astype(jnp.bfloat16), "dp", scatter_dimension=0, tiled=True
        ).astype(jnp.float32),
        lax.psum_scatter(
            gain_grads.astype(jnp.bfloat16), "dp", scatter_dimension=1, tiled=True
        ).astype(jnp.float32),
    )
    owned_w, owned_g = (
        lax.psum(owned_w.astype(jnp.bfloat16), "seq").astype(jnp.float32),
        lax.psum(owned_g.astype(jnp.bfloat16), "seq").astype(jnp.float32),
    )
    scale_grad = lax.psum(scale_part, ("dp", "seq")) * base_scale * jax.nn.sigmoid(qscale)
    weights_new, weight_m_new, weight_v_new = adamw(
        weights, owned_w, weight_m, weight_v, RATE_MATRIX
    )
    gains_new, gain_m_new, gain_v_new = adamw(gains, owned_g, gain_m, gain_v, RATE_GAIN)
    qscale_new, qscale_m_new, qscale_v_new = adamw(
        qscale, scale_grad, qscale_m, qscale_v, RATE_GAIN
    )
    return (
        outputs[None],
        input_grad[None],
        weights_new,
        weight_m_new,
        weight_v_new,
        weights_new.astype(jnp.bfloat16),
        gains_new,
        gain_m_new,
        gain_v_new,
        qscale_new,
        qscale_m_new,
        qscale_v_new,
    )


def solution(mesh):
    placed = (
        P("dp", "seq", None),
        P("dp", "seq", None),
        P("dp", None),
        P("dp", None),
        P("dp", None),
        P("dp", None),
        P(None, "dp"),
        P(None, "dp"),
        P(None, "dp"),
        P(),
        P(),
        P(),
    )
    return jax.shard_map(
        on_device,
        mesh=mesh,
        in_specs=placed,
        out_specs=(
            P("dp", "seq", None),
            P("dp", "seq", None),
            P("dp", None),
            P("dp", None),
            P("dp", None),
            P("dp", None),
            P(None, "dp"),
            P(None, "dp"),
            P(None, "dp"),
            P(),
            P(),
            P(),
        ),
        check_vma=False,
    )
```

profile of v0, /device:TPU:0, one launch (start us, length us, event | category | flops | bytes accessed | tf_op | source)
XLA Modules:
  0.0 665.3 jit_solution(17955789964607941840)
XLA Ops:
  10.4 23.0 %all-gather = bf16[16,80,2]{1,2,0:T(2,128)(2,1)S(1)} all-gather(bf16[1,80,2]{1,2,0:T(2,128)(2,1)S(1)} %convert_bitcast_fusion), channel_id=1, replica_groups=mesh['dp'=16,'seq'=2] {'dp'}, dimensions={0}, use_global_device_ids=true | all-gather | bytes 5440 | tf_op jit(solution)/shard_map/all_gather | solution.py:63
  33.7 82.0 %all-gather.3.cloned.1.call-done = bf16[1280,7680]{1,0:T(8,128)(2,1)} async-done(((bf16[80,7680]{1,0:T(8,128)(2,1)}), bf16[1280,7680]{1,0:T(8,128)(2,1)}) %all-gather.3.cloned.1.call-update) | async-done | bytes 19660816 | tf_op jit(solution)/shard_map/all_gather | solution.py:62
  115.8 8.1 %slice_bitcast_fusion = bf16[3840,1280]{0,1:T(8,128)(2,1)} fusion(bf16[1280,7680]{1,0:T(8,128)(2,1)} %all-gather.3.cloned.1.call-done), kind=kLoop, calls=%fused_computation.4 | loop fusion | bytes 19660800 | tf_op jit(solution)/shard_map/dot_general | solution.py:82
  123.9 13.8 %copy.100 = bf16[3840,1280]{1,0:T(8,128)(2,1)} copy(bf16[3840,1280]{0,1:T(8,128)(2,1)} %slice_bitcast_fusion) | data formatting | bytes 19660800 | tf_op jit(solution)/shard_map/dot_general | solution.py:82
  137.6 8.4 %multiply_convert_fusion.1 = (bf16[256,3,1280]{2,0,1:T(8,128)(2,1)S(1)}, f32[256,3,1280]{2,0,1:T(8,128)}) fusion(f32[3,1280]{1,0:T(4,128)S(1)} %stack.20, bf16[3,1280,1280]{2,1,0:T(8,128)(2,1)} %bitcast.115, f32[1280]{0:T(1024)S(1)} %get-tuple-element.63, f32[1,256,1280]{2,1,0:T(8,128)S(1)} %copy-done.1, f32[256]{0:T(256)S(1)} %add_rsqrt_fusion.1), kind=kOutput, calls=%fused_computation.21 | convolution fusion | flops 2519531520 | bytes 17060864 | tf_op jit(solution)/shard_map/dot_general | solution.py:82
  149.3 5.2 all-to-all-start
  154.8 30.9 %all-to-all-done = bf16[256,3,1280]{0,1,2:T(4,128)(2,1)} async-done(((bf16[256,3,1280]{0,1,2:T(4,128)(2,1)}), bf16[256,3,1280]{0,1,2:T(4,128)(2,1)}, u32[]{:S(2)}, u32[]{:S(2)}) %all-to-all-start) | async-done | bytes 1966112 | tf_op jit(solution)/shard_map/all_to_all | solution.py:89
  207.4 12.0 %all_to_all.71 = bf16[2,256,640]{1,2,0:T(8,128)(2,1)S(1)} all-to-all(bf16[2,256,640]{1,2,0:T(8,128)(2,1)S(1)} %copy.108), channel_id=1, replica_groups=mesh['dp'=16,'seq'=2] {'seq'}, dimensions={0} | all-to-all | bytes 1310720 | tf_op jit(solution)/shard_map/all_to_all | solution.py:115
  243.9 7.0 %all-to-all-done.2 = bf16[256,2,640]{2,0,1:T(8,128)(2,1)S(1)} async-done(((bf16[256,2,640]{2,0,1:T(8,128)(2,1)}), bf16[256,2,640]{2,0,1:T(8,128)(2,1)S(1)}, u32[]{:S(2)}, u32[]{:S(2)}) %all-to-all-start.2) | async-done | bytes 655392 | tf_op jit(solution)/shard_map/all_to_all | solution.py:134
  252.3 6.3 fusion.45
  258.6 4.9 multiply_reduce_fusion
  275.3 6.4 pad_maximum_fusion.1
  281.7 5.0 all-to-all-start.3
  295.6 19.7 %all-to-all-done.3 = bf16[512,3,640]{2,1,0:T(4,128)(2,1)} async-done(((bf16[512,3,640]{2,1,0:T(4,128)(2,1)}), bf16[512,3,640]{2,1,0:T(4,128)(2,1)}, u32[]{:S(2)}, u32[]{:S(2)}) %all-to-all-start.3) | async-done | bytes 1966112 | tf_op jit(solution)/shard_map/all_to_all | solution.py:176
  325.1 8.6 %convolution_convert_fusion = bf16[1280,3840]{1,0:T(8,128)(2,1)} fusion(bf16[256,3840]{0,1:T(8,128)(2,1)} %bitcast.121, f32[1,256,1280]{2,1,0:T(8,128)} %param.12, f32[1280]{0:T(1024)S(1)} %get-tuple-element.63, f32[256]{0:T(256)S(1)} %copy-done.25), kind=kOutput, calls=%fused_computation.1 | convolution fusion | flops 2522480640 | bytes 13113344 | tf_op jit(solution)/shard_map/dot_general | solution.py:183
  333.7 14.8 %pad_maximum_fusion = bf16[1280,7680]{1,0:T(8,128)(2,1)} fusion(bf16[1280,1280]{1,0:T(8,128)(2,1)} %convolution_convert_fusion.1, bf16[1280,1280]{1,0:T(8,128)(2,1)} %convolution_convert_fusion.2, bf16[1280,1280]{1,0:T(8,128)(2,1)S(1)} %convolution_convert_fusion.3, bf16[1280,3840]{1,0:T(8,128)(2,1)} %convolution_convert_fusion), kind=kLoop, calls=%fused_computation | loop fusion | flops 78643200 | bytes 39321600 | tf_op jit(solution)/shard_map/concatenate | solution.py:187
  350.4 8.5 %multiply_reduce_fusion.2 = (bf16[1280]{0:T(1024)(128)(2,1)S(1)}, f32[256]{0:T(256)S(1)}, f32[256,1280]{1,0:T(8,128)}) fusion(f32[1,256,1280]{2,1,0:T(8,128)S(1)} %copy-done.2, f32[256]{0:T(256)S(1)} %copy-done.25, f32[1280]{0:T(1024)S(1)} %get-tuple-element.63, bf16[256,3840]{0,1:T(8,128)(2,1)S(1)} %bitcast.122, ...), kind=kOutput, calls=%fused_computation.61 | convolution fusion | flops 2518546944 | bytes 14427648 | tf_op jit(solution)/shard_map/dot_general | solution.py:184
  360.3 6.3 fusion.34
  366.7 40.5 %psum.23 = f32[80]{0:T(128)S(1)} all-reduce(f32[80]{0:T(128)S(1)} %reduce_sum.111), channel_id=1, replica_groups=mesh['dp'=16,'seq'=2] {'dp','seq'}, use_global_device_ids=true, to_apply=%region_16.17 | all-reduce | flops 80 | bytes 640 | tf_op jit(solution)/shard_map/psum | solution.py:201
  407.2 141.7 %reduce-scatter.5.cloned.1.call-done = bf16[80,7680]{1,0:T(8,128)(2,1)} async-done(((bf16[1280,7680]{1,0:T(8,128)(2,1)}), bf16[80,7680]{1,0:T(8,128)(2,1)}) %reduce-scatter.5.cloned.1.call-update) | async-done | bytes 1228816 | tf_op jit(solution)/shard_map/reduce_scatter | solution.py:190
  552.3 52.9 %reduce-scatter.7.cloned.1.call-done = bf16[80,2]{1,0:T(8,128)(2,1)} async-done(((bf16[1280,2]{1,0:T(8,128)(2,1)}), bf16[80,2]{1,0:T(8,128)(2,1)}) %reduce-scatter.7.cloned.1.call-update) | async-done | bytes 336
  606.0 4.9 psum.22
  611.5 38.9 %all-reduce.3.cloned.1.call-done = bf16[80,7680]{1,0:T(8,128)(2,1)} async-done(((bf16[80,7680]{1,0:T(8,128)(2,1)}), bf16[80,7680]{1,0:T(8,128)(2,1)}) %all-reduce.3.cloned.1.call-update) | async-done | bytes 1228816 | tf_op jit(solution)/shard_map/psum | solution.py:198
  650.4 8.2 %fusion.69 = (bf16[80,7680]{1,0:T(8,128)(2,1)}, f32[80,7680]{1,0:T(8,128)}, f32[80,7680]{1,0:T(8,128)}, f32[80,7680]{1,0:T(8,128)}) fusion(f32[80,7680]{1,0:T(8,128)} %param.15, bf16[80,7680]{1,0:T(8,128)(2,1)} %all-reduce.3.cloned.1.call-done, f32[80,7680]{1,0:T(8,128)} %param.16, f32[80,7680]{1,0:T(8,128)} %param.17), kind=kLoop, calls=%fused_computation.106 | loop fusion | flops 9830400 | bytes 17203200 | tf_op jit(solution)/shard_map/convert_element_type | solution.py:215
  (159 shorter events, 92.6 us)
Async XLA Ops:
  7.2 26.3 %copy-start.1 = (f32[1,256,1280]{2,1,0:T(8,128)S(1)}, f32[1,256,1280]{2,1,0:T(8,128)}, u32[]{:S(2)}) copy-start(f32[1,256,1280]{2,1,0:T(8,128)} %param.12) | copy-start | bytes 3932164
  7.2 108.5 %all-gather.3.cloned.1.call-start = ((), (), s32[]{:S(2)}) async-start(), calls=%async_computation.6 | async-start | bytes 20889600 | tf_op jit(solution)/shard_map/all_gather | solution.py:62
  10.3 113.6 %copy-start.19 = (f32[16,80]{1,0:T(8,128)}, f32[16,80]{1,0:T(8,128)S(1)}, u32[]{:S(2)}) copy-start(f32[16,80]{1,0:T(8,128)S(1)} %tile.2) | copy-start | bytes 15364
  33.7 103.9 %copy-start.24 = (f32[256]{0:T(256)}, f32[256]{0:T(256)S(1)}, u32[]{:S(2)}) copy-start(f32[256]{0:T(256)S(1)} %add_rsqrt_fusion.1) | copy-start | bytes 3076
  149.3 5.2 copy-start.33
  149.3 36.4 %all-to-all-start = ((bf16[256,3,1280]{0,1,2:T(4,128)(2,1)}), bf16[256,3,1280]{0,1,2:T(4,128)(2,1)}, u32[]{:S(2)}, u32[]{:S(2)}) async-start(bf16[256,3,1280]{0,1,2:T(4,128)(2,1)} %copy.101), calls=%async_computation | async-start | bytes 5242880 | tf_op jit(solution)/shard_map/all_to_all | solution.py:89
  194.5 5.8 copy-start.9
  222.7 11.6 %copy-start.6 = (f32[256,1280]{1,0:T(8,128)}, f32[256,1280]{1,0:T(8,128)S(1)}, u32[]{:S(2)}) copy-start(f32[256,1280]{1,0:T(8,128)S(1)} %get-tuple-element.95) | copy-start | bytes 3932164
  222.7 11.6 %copy-start.26 = (f32[256]{0:T(256)}, f32[256]{0:T(256)S(1)}, u32[]{:S(2)}) copy-start(f32[256]{0:T(256)S(1)} %add_rsqrt_fusion) | copy-start | bytes 3076
  239.1 11.8 %all-to-all-start.2 = ((bf16[256,2,640]{2,0,1:T(8,128)(2,1)}), bf16[256,2,640]{2,0,1:T(8,128)(2,1)S(1)}, u32[]{:S(2)}, u32[]{:S(2)}) async-start(bf16[256,2,640]{2,0,1:T(8,128)(2,1)} %bitcast.112), calls=%async_computation.2 | async-start | bytes 1310720 | tf_op jit(solution)/shard_map/all_to_all | solution.py:134
  252.3 6.3 copy-start.10
  252.3 6.3 copy-start.18
  252.3 11.2 %slice-start = ((s8[8388608]{0:T(1024)(128)(4,1)}), s8[4194304]{0:T(1024)(128)(4,1)S(1)}, s32[]{:S(2)}) async-start(s8[8388608]{0:T(1024)(128)(4,1)} %bitcast.113), calls=%async_computation.10 | async-start | bytes 8388608
  281.7 33.6 %all-to-all-start.3 = ((bf16[512,3,640]{2,1,0:T(4,128)(2,1)}), bf16[512,3,640]{2,1,0:T(4,128)(2,1)}, u32[]{:S(2)}, u32[]{:S(2)}) async-start(bf16[512,3,640]{2,1,0:T(4,128)(2,1)} %pad_maximum_fusion.1), calls=%async_computation.3 | async-start | bytes 5242880 | tf_op jit(solution)/shard_map/all_to_all | solution.py:176
  286.7 262.2 %reduce-scatter.5.cloned.1.call-start = ((), (), s32[]{:S(2)}) async-start(), calls=%async_computation.7 | async-start | bytes 20889600 | tf_op jit(solution)/shard_map/reduce_scatter | solution.py:190
  348.5 256.6 %reduce-scatter.7.cloned.1.call-start = ((), (), s32[]{:S(2)}) async-start(), calls=%async_computation.9 | async-start | bytes 348160
  360.0 189.0 %copy-start.35 = (f32[80]{0:T(128)S(1)}, f32[80]{0:T(128)}, u32[]{:S(2)}) copy-start(f32[80]{0:T(128)} %param.21) | copy-start | bytes 964
  360.0 189.0 %copy-start.36 = (f32[80]{0:T(128)S(1)}, f32[80]{0:T(128)}, u32[]{:S(2)}) copy-start(f32[80]{0:T(128)} %param.22) | copy-start | bytes 964
  360.0 189.0 %copy-start.37 = (f32[80]{0:T(128)S(1)}, f32[80]{0:T(128)}, u32[]{:S(2)}) copy-start(f32[80]{0:T(128)} %param.23) | copy-start | bytes 964
  360.0 290.4 %all-reduce.3.cloned.1.call-start = ((), (), s32[]{:S(2)}) async-start(), calls=%async_computation.8 | async-start | bytes 2457600 | tf_op jit(solution)/shard_map/psum | solution.py:198
  360.3 189.3 %copy-start.4 = (f32[256,1280]{1,0:T(8,128)S(1)}, f32[256,1280]{1,0:T(8,128)}, u32[]{:S(2)}) copy-start(f32[256,1280]{1,0:T(8,128)} %copy-done.3) | copy-start | bytes 3932164
  549.6 61.3 %copy-start.30 = (f32[2,80]{1,0:T(2,128)S(1)}, f32[2,80]{1,0:T(2,128)}, u32[]{:S(2)}) copy-start(f32[2,80]{1,0:T(2,128)} %param.18) | copy-start | bytes 1924
  549.6 61.3 %copy-start.31 = (f32[2,80]{1,0:T(2,128)S(1)}, f32[2,80]{1,0:T(2,128)}, u32[]{:S(2)}) copy-start(f32[2,80]{1,0:T(2,128)} %param.19) | copy-start | bytes 1924
  549.6 61.3 %copy-start.32 = (f32[2,80]{1,0:T(2,128)S(1)}, f32[2,80]{1,0:T(2,128)}, u32[]{:S(2)}) copy-start(f32[2,80]{1,0:T(2,128)} %param.20) | copy-start | bytes 1924
  (25 other events, 75.4 us)
Sparse Core Ops, SparseCore 0:
  10.3 105.3 all-gather.2
  348.7 200.2 reduce-scatter.4
  553.0 52.1 reduce-scatter.6
  607.3 43.0 all-reduce.2
where the time goes:
time: 675 us; the launch traced here: 665 us
  waiting for transfers between devices  373 us (55%)
  blocking collectives  80.5 us (12%)
  matrix products  76.3 us (11%)
  local copies, waits for them, and re-layouts  61.6 us (9%)
  other arithmetic  44.8 us (7%)
  between operations  14.7 us (2%)
  starting transfers between devices  14.2 us (2%)
    reduce_scatter x1, waiting for transfers between devices, on_device(): lax.psum_scatter(all_grads.astype(jnp.bfloat16), 'dp', scatter_dimension=...  142 us
    all_gather x1, waiting for transfers between devices, on_device(): lax.all_gather(weights.astype(jnp.bfloat16), 'dp', axis=0, tiled=True)  82 us
    unnamed x5, waiting for transfers between devices  52.9 us
    psum x1, blocking collectives, on_device(): lax.psum(scale_part, ('dp', 'seq')) * base_scale * jax.nn.sigmoid(qscale)  40.5 us
    psum x1, waiting for transfers between devices, on_device(): lax.psum(owned_w.astype(jnp.bfloat16), 'seq').astype(jnp.float32)  38.9 us
    all_to_all x1, waiting for transfers between devices, on_device(): lax.all_to_all(outgoing, 'seq', split_axis=2, concat_axis=0, tiled=True)  30.9 us
    all_gather x1, blocking collectives, on_device(): lax.all_gather(gains.astype(jnp.bfloat16), 'dp', axis=1, tiled=True)  23 us
    dot_general x2, local copies, waits for them, and re-layouts, on_device(): jnp.dot(hidden_one, w_qkv, preferred_element_type=jnp.float32)  21.9 us
  transfers between devices with their start and end apart: 7, of which 7 were waited for; matrix products, arithmetic and copies ran while one was open for 5% of the time, Pallas kernels for 0%

commit v1 on v0

--- a/solution.py
+++ b/solution.py
@@ -1,8 +1,12 @@
+import functools
 import math
+import types
 
 import jax
 import jax.numpy as jnp
 from jax import lax
+from jax.experimental import pallas as pl
+from jax.experimental.pallas import tpu as pltpu
 from jax.sharding import PartitionSpec as P
 
 HEADS = 16
@@ -44,7 +48,7 @@
     return (param_new, first_new, second_new)
 
 
-def on_device(
+def plain_layer(
     inputs,
     cotangent,
     starts,
@@ -222,6 +226,1029 @@
     )
 
 
+MESH = pl.DeviceIdType.MESH
+BF = jnp.bfloat16
+F32 = jnp.float32
+DEPTH = 4
+STEP_ROWS = 32
+UNITS = 8
+TREE = ("o", "O", "d", "D")
+VMEM_BYTES = 64 * 1024 * 1024
+
+
+class Hop:
+    def __init__(self, number, sems, source, target, arriving, device, when=None, into=None):
+        self.number, self.when, self.pending = number, when, True
+        self.out = self.describe(number, into or number, sems, source, target, device)
+        if arriving is not None:
+            self.back = self.describe(number, number, sems, arriving, arriving, device)
+        self.guard(self.out.start)
+
+    @staticmethod
+    def describe(number, into, sems, source, target, device):
+        return pltpu.make_async_remote_copy(
+            src_ref=source,
+            dst_ref=target,
+            send_sem=sems[0].at[number],
+            recv_sem=sems[1].at[into],
+            device_id=device,
+            device_id_type=MESH,
+        )
+
+    def guard(self, action):
+        if self.when is None:
+            action()
+        else:
+            pl.when(self.when)(action)
+
+    def arrived(self):
+        self.back.wait_recv()
+
+    def left(self):
+        if self.pending:
+            self.guard(self.out.wait_send)
+        self.pending = False
+
+
+def dot_nn(left, right):
+    return lax.dot_general(left, right, (((1,), (0,)), ((), ())), preferred_element_type=F32)
+
+
+def dot_nt(left, right):
+    return lax.dot_general(left, right, (((1,), (1,)), ((), ())), preferred_element_type=F32)
+
+
+def dot_tn(left, right):
+    return lax.dot_general(left, right, (((0,), (0,)), ((), ())), preferred_element_type=F32)
+
+
+def inverse_rms(rows):
+    return lax.rsqrt(jnp.mean(rows * rows, axis=-1, keepdims=True) + EPS)
+
+
+def loop(count, body):
+    def step(index, carry):
+        body(index)
+        return carry
+
+    lax.fori_loop(0, count, step, 0)
+
+
+def scratch_plan(count, width, half, rows):
+    length = 2 * count
+    blocks = (DEPTH, 2, 2, rows, half)
+    return dict(
+        x=((count, width), F32),
+        x2=((count, width), F32),
+        cd=((count, width), F32),
+        dh=((count, width), F32),
+        qf=((length, half), F32),
+        h1=((length, width), BF),
+        gb=((2, count, width), BF),
+        du=((2, count, width), BF),
+        ab=((2, count, half), BF),
+        abh=((2, length, half), BF),
+        of=((2, length, half), BF),
+        dos=((count, half), BF),
+        dof=((length, half), BF),
+        qkv=((3, length, half), BF),
+        dq=((2, 3, length, half), BF),
+        tz=((2 * DEPTH, 2, rows, count), BF),
+        th=((2 * DEPTH, 2, rows, count), BF),
+        to=((2 * DEPTH, 2, rows, length), BF),
+        tzr=((2 * DEPTH, rows, count), BF),
+        thr=((2 * DEPTH, rows, count), BF),
+        tor=((2 * DEPTH, rows, length), BF),
+        t1=((2 * DEPTH, 2, rows, length), BF),
+        t1r=((2 * DEPTH, rows, length), BF),
+        bias=((length, length), F32),
+        p0=((8, count, count), BF),
+        p1=((8, length, count), BF),
+        dh1r=((count, width), BF),
+        wst=((UNITS, rows, half), F32),
+        w=((9,) + blocks, BF),
+        s=((8, DEPTH, 2, rows, half), BF),
+        yr=((DEPTH, 2, rows, half), BF),
+        xr=((7, DEPTH, rows, half), BF),
+        zr=((7, DEPTH - 1, rows, half), BF),
+        g=((12, rows, half), BF),
+        go=((2, rows, half), BF),
+        gr=((2, rows, half), BF),
+        gn=((DEPTH, 2, 2, rows, 128), BF),
+        gs=((128, 128), F32),
+        fs=((8, half), F32),
+        gt=((8, width), F32),
+        dg=((2, 8, width), F32),
+        sm=((4, 8, width), F32),
+        smr=((3, 8, width), F32),
+        smz=((DEPTH, 8, width), F32),
+    )
+
+
+HOPS = 168
+ORDER = (
+    "gz", "stv", "stk", "sto", "oxv", "stO", "std", "stq", "gx", "stD", "bias", "stup", "gb",
+    "fzv1", "gc", "fzv2", "h1", "fzv3", "fcv", "oxk", "fzk1", "fxv", "fzk2", "fzk3", "fck", "oxq",
+    "fzq1", "fxk", "fzq2", "h1_", "Pv", "Pk", "fzq3", "oxup", "t1", "fcq", "fzup1", "fxq", "fzup2",
+    "fzup3", "zao", "zaO", "zad", "szD", "Pq", "A0", "fxup", "A1", "zio", "A2", "zaD", "A3", "A4",
+    "ziO", "A5", "A6", "zbo", "A7", "zid", "so", "fcup", "zbO", "fxo", "zbd", "ziD", "fyup", "fxO",
+    "fxd", "x2", "h2", "u", "zbD", "th", "tz", "to", "dz", "dh2", "dx2", "do0", "Wd", "do1", "out",
+    "Wup", "axd01", "axd02", "B0", "axd03", "B1", "B2", "axd11", "abc", "B3", "axd12", "B4",
+    "axd13", "axd10", "Wo", "B5", "B6", "axo1", "B7", "axo2", "dvk", "dq", "axo3", "axd00", "azd0",
+    "ayup", "Wv", "Wk", "axup1", "aed0", "Wq", "axup2", "axo0", "azo", "axup3", "dhp", "dho",
+    "aeo", "axv1", "axup0", "azd1", "axv2", "azup", "axv3", "axv0", "axk1", "axk2", "axk3", "azv",
+    "ig", "axk0", "aed1", "axq1", "smx", "aeup", "axq2", "aev", "axq3", "azk", "axq0", "smy",
+    "aek", "smz", "azq", "sme", "aeq",
+)
+
+
+def layer_kernel(
+    names, head_dim, x_hbm, cot_hbm, starts, w_hbm, gains_own, qscale,
+    out_hbm, grad_in_hbm, grad_hbm, small_hbm, *scratch
+):
+    m = types.SimpleNamespace(**dict(zip(names, scratch[: len(names)])))
+    send_sems, recv_sems, load_sems, store_sems = scratch[len(names):]
+    sems = (send_sems, recv_sems)
+    count, width = m.x.shape
+    length, half = m.dof.shape
+    rows = m.wst.shape[1]
+    heads = half // head_dim
+
+    me = lax.axis_index("dp")
+    y = lax.axis_index("seq")
+    z = lax.div(me, 4)
+    x = lax.rem(lax.div(me, 2), 2)
+    c = lax.rem(me, 2)
+    oy, ox, oc = 1 - y, 1 - x, 1 - c
+    to_y = {"seq": oy}
+    to_x = {"dp": 4 * z + 2 * ox + c}
+    to_c = {"dp": 4 * z + 2 * x + oc}
+    up_z = [lax.rem(z + k, DEPTH) for k in range(DEPTH)]
+    down_z = [lax.rem(z + DEPTH - k, DEPTH) for k in range(DEPTH)]
+    to_z = [{"dp": 4 * up_z[k] + 2 * x + c} for k in range(DEPTH)]
+    inner = (z == 1) | (z == 2)
+    near_z = z + 1 - 2 * lax.rem(z, 2)
+    to_near = {"dp": 4 * near_z + 2 * x + c}
+    to_middle = {"dp": 4 * (DEPTH - 1 - z) + 2 * x + c}
+    near = pl.ds(2 * lax.div(z, 2), 2)
+    far = pl.ds(2 - 2 * lax.div(z, 2), 2)
+    hops = []
+
+    def send(source, target, arriving, device, when=None, into=None):
+        one = Hop(len(hops), sems, source, target, arriving, device, when, into)
+        hops.append(one)
+        return one
+
+    own_row = pl.multiple_of(y * count, count)
+    peer_row = pl.multiple_of(oy * count, count)
+
+    names_of = ["v", "k", "q", "up", "o", "O", "d", "D"]
+    unit_part = [2, 1, 0, 4, 3, 3, 5, 5]
+    unit_half = [y, y, y, y, y, oy, y, oy]
+    unit_slot = [2, 1, 0, 5 + y, 3 + y, 3 + oy, 7 + y, 7 + oy]
+    swap_slot = 5 + oy
+    loads = []
+    for u in range(UNITS):
+        start = pl.multiple_of(unit_part[u] * width + unit_half[u] * half, 128)
+        loads.append(
+            pltpu.make_async_copy(w_hbm.at[:, pl.ds(start, half)], m.wst.at[u], load_sems.at[u])
+        )
+        loads[u].start()
+    load_x = pltpu.make_async_copy(x_hbm, m.x, load_sems.at[UNITS])
+    load_cot = pltpu.make_async_copy(cot_hbm, m.cd, load_sems.at[UNITS + 1])
+    load_x.start()
+    load_cot.start()
+    steps = {}
+
+    def step(name):
+        def keep(body):
+            steps[name] = body
+            return body
+
+        return keep
+
+    barrier = pltpu.get_barrier_semaphore()
+    for device in (to_y, to_x, to_c, to_z[1], to_z[2], to_z[3]):
+        pl.semaphore_signal(barrier, inc=1, device_id=device, device_id_type=MESH)
+    m.gs[...] = jnp.zeros_like(m.gs)
+    m.gs[0:2, 0:rows] = gains_own[...]
+    m.gn[z, x, c] = jnp.transpose(m.gs[...])[:rows].astype(BF)
+    stretch = jnp.maximum(qscale[...], 0.0) + jnp.log1p(jnp.exp(-jnp.abs(qscale[...])))
+    m.fs[...] = jnp.zeros_like(m.fs)
+    m.fs[0:1, 0:head_dim] = QUERY_BASE / math.sqrt(head_dim) * stretch
+    one_head = m.fs[...]
+    every = one_head
+    for head in range(1, heads):
+        every = every + pltpu.roll(one_head, head * head_dim, 1)
+    m.fs[...] = every
+    factor = m.fs.at[0:1]
+    pl.semaphore_wait(barrier, 6)
+
+    hop = {}
+
+    @step("gz")
+    def _():
+        block = m.gn.at[z, x, c]
+        for k in range(1, DEPTH):
+            hop["gz", k] = send(block, block, m.gn.at[down_z[k], x, c], to_z[k])
+
+    @step("gx")
+    def _():
+        for k in range(1, DEPTH):
+            hop["gz", k].arrived()
+        block = m.gn.at[:, x, c]
+        hop["gx"] = send(block, block, m.gn.at[:, ox, c], to_x)
+
+    @step("gc")
+    def _():
+        hop["gx"].arrived()
+        block = m.gn.at[:, :, c]
+        hop["gc"] = send(block, block, m.gn.at[:, :, oc], to_c)
+
+    @step("gb")
+    def _():
+        load_cot.wait()
+
+        def make_gb(index):
+            at = pl.ds(index * STEP_ROWS, STEP_ROWS)
+            m.gb[0, at] = m.cd[at].astype(BF)
+
+        loop(count // STEP_ROWS, make_gb)
+        hop["gb"] = send(m.gb.at[0], m.gb.at[1], m.gb.at[1], to_c)
+
+    @step("bias")
+    def _():
+        position = lax.broadcasted_iota(jnp.int32, (1, length), 1)
+        begin = jnp.zeros((1, length), jnp.int32)
+        for j in range(starts.shape[1]):
+            begin = jnp.maximum(begin, jnp.where(starts[0, j] <= position, starts[0, j], 0))
+
+        def make_bias(index):
+            key = lax.broadcasted_iota(jnp.int32, (STEP_ROWS, length), 0) + index * STEP_ROWS
+            kept = (key <= position) & (key >= begin)
+            m.bias[pl.ds(index * STEP_ROWS, STEP_ROWS)] = jnp.where(kept, 0.0, NEG)
+
+        loop(length // STEP_ROWS, make_bias)
+        m.of[y] = jnp.zeros_like(m.of[y])
+        m.dq[0] = jnp.zeros_like(m.dq[0])
+        m.dg[...] = jnp.zeros_like(m.dg)
+
+    h1_own, h1_peer = m.h1.at[pl.ds(own_row, count)], m.h1.at[pl.ds(peer_row, count)]
+
+    @step("h1")
+    def _():
+        load_x.wait()
+        hop["gc"].arrived()
+        gains = m.gn[...].reshape(width, 128).astype(F32)
+        m.gt[...] = jnp.transpose(gains)[:8]
+
+        def make_h1(index):
+            values = m.x[pl.ds(index * STEP_ROWS, STEP_ROWS)]
+            normed = values * inverse_rms(values)
+            at = pl.ds(pl.multiple_of(own_row + index * STEP_ROWS, STEP_ROWS), STEP_ROWS)
+            m.h1[at] = (normed * m.gt[0:1]).astype(BF)
+
+        loop(count // STEP_ROWS, make_h1)
+        hop["h1"] = send(h1_own, h1_own, h1_peer, to_y)
+
+    def unit_steps(u):
+        name, slot = names_of[u], unit_slot[u]
+
+        @step("st" + name)
+        def _():
+            loads[u].wait()
+            m.w[slot, z, x, c] = m.wst[u].astype(BF)
+            block = m.w.at[slot, z, x, c]
+            for k in range(1, DEPTH):
+                hop["z", u, k] = send(block, block, m.w.at[slot, down_z[k], x, c], to_z[k])
+
+        def forward(k):
+            def body():
+                if k:
+                    hop["z", u, k].arrived()
+                block = m.w.at[slot, down_z[k], x, c]
+                hop["x", u, k] = send(block, block, m.w.at[slot, down_z[k], ox, c], to_x)
+
+            return body
+
+        steps["ox" + name] = forward(0)
+        for k in range(1, DEPTH):
+            steps[f"fz{name}{k}"] = forward(k)
+
+        @step("fc" + name)
+        def _():
+            block = m.w.at[slot, :, x, c]
+            hop["c", u, 0] = send(block, block, m.w.at[slot, :, x, oc], to_c)
+
+        @step("fx" + name)
+        def _():
+            for k in range(DEPTH):
+                hop["x", u, k].arrived()
+            if name == "up":
+                block = m.w.at[slot, :, :, c]
+                hop["y", u] = send(block, block, m.w.at[swap_slot, :, :, c], to_y)
+            block = m.w.at[slot, :, ox, c]
+            hop["c", u, 1] = send(block, block, m.w.at[slot, :, ox, oc], to_c)
+
+        @step("fy" + name)
+        def _():
+            hop["y", u].arrived()
+            block = m.w.at[swap_slot, :, :, c]
+            hop["yc", u] = send(block, block, m.w.at[swap_slot, :, :, oc], to_c)
+
+    def tree_steps(u, first_x):
+        name, slot = names_of[u], unit_slot[u]
+        side = slice(None) if first_x else x
+
+        def pair_start():
+            block = m.w.at[slot, z, side, c]
+            hop["za", u] = send(block, block, m.w.at[slot, near_z, side, c], to_near)
+
+        @step("st" + name)
+        def _():
+            loads[u].wait()
+            m.w[slot, z, x, c] = m.wst[u].astype(BF)
+            if first_x:
+                block = m.w.at[slot, z, x, c]
+                hop["xo", u] = send(block, block, m.w.at[slot, z, ox, c], to_x)
+            else:
+                pair_start()
+
+        @step("sz" + name)
+        def _():
+            hop["xo", u].arrived()
+            pair_start()
+
+        @step("za" + name)
+        def _():
+            hop["za", u].arrived()
+            block = m.w.at[slot, near, side, c]
+            hop["zb", u] = send(
+                block, block, m.w.at[slot, far, side, c], to_middle, when=inner
+            )
+            if not first_x:
+                hop["xa", u] = send(block, block, m.w.at[slot, near, ox, c], to_x)
+
+        @step("zi" + name)
+        def _():
+            pl.when(inner)(hop["zb", u].arrived)
+            block = m.w.at[slot, far, side, c]
+            hop["zc", u] = send(
+                block, block, None, to_near, when=inner, into=hop["zb", u].number
+            )
+
+        @step("zb" + name)
+        def _():
+            pl.when(jnp.logical_not(inner))(hop["zb", u].arrived)
+            if first_x:
+                block = m.w.at[slot, :, :, c]
+                hop["c", u, 1] = send(block, block, m.w.at[slot, :, :, oc], to_c)
+                return
+            block = m.w.at[slot, far, x, c]
+            hop["xb", u] = send(block, block, m.w.at[slot, far, ox, c], to_x)
+            block = m.w.at[slot, :, x, c]
+            hop["c", u, 0] = send(block, block, m.w.at[slot, :, x, oc], to_c)
+
+        @step("fx" + name)
+        def _():
+            hop["xa", u].arrived()
+            hop["xb", u].arrived()
+            block = m.w.at[slot, :, ox, c]
+            hop["c", u, 1] = send(block, block, m.w.at[slot, :, ox, oc], to_c)
+
+    for u in range(UNITS):
+        if names_of[u] in TREE:
+            tree_steps(u, names_of[u] == TREE[-1])
+        else:
+            unit_steps(u)
+
+    def ready(*wanted):
+        for name in wanted:
+            u = names_of.index(name)
+            if ("c", u, 0) in hop:
+                hop["c", u, 0].arrived()
+            hop["c", u, 1].arrived()
+            if name == "up":
+                hop["yc", u].arrived()
+
+    def weight(slot):
+        return m.w[slot].reshape(width, half)
+
+    def project(part):
+        def block(index):
+            at = pl.ds(pl.multiple_of(index * count, count), count)
+            result = dot_nn(m.h1[at], weight(part))
+            if part == 0:
+                m.qf[at] = result
+                result = result * factor[...]
+            m.qkv[part, at] = result.astype(BF)
+
+        loop(2, block)
+
+    @step("t1")
+    def _():
+        def transpose_h1(index):
+            at = pl.ds(pl.multiple_of(index * count, count), count)
+            m.t1[:, :, :, at] = jnp.transpose(m.h1[at]).reshape(2 * DEPTH, 2, rows, count)
+
+        loop(2, transpose_h1)
+        hop["t1"] = send(m.t1.at[:, oc], m.t1r, m.t1r, to_c)
+
+    def project_step(name):
+        def body():
+            ready(name)
+            project("qkv".index(name))
+
+        return body
+
+    for name in "qkv":
+        steps["P" + name] = project_step(name)
+
+    def head_window(head):
+        first = min(head * head_dim // 128 * 128, half - 256)
+        lane = lax.broadcasted_iota(jnp.int32, (1, 256), 1) + first
+        inside = (lane >= head * head_dim) & (lane < (head + 1) * head_dim)
+        return slice(first, first + 256), jnp.where(inside, 1.0, 0.0).astype(BF)
+
+    def attend(head):
+        window, mask = head_window(head)
+        keys = m.qkv[1, :, window]
+        queries = m.qkv[0, :, window] * mask
+        values = m.qkv[2, :, window] * mask
+        for b in range(2):
+            at, upto = slice(b * count, (b + 1) * count), (b + 1) * count
+            scores = dot_nt(keys[:upto], queries[at]) + m.bias[:upto, at]
+            top = jnp.max(scores, axis=0, keepdims=True)
+            expo = jnp.exp(scores - top)
+            total = jnp.sum(expo, axis=0, keepdims=True)
+            probs = (expo * (1.0 / total)).astype(BF)
+            kept = m.p1 if b else m.p0
+            kept[head] = probs
+            found = dot_tn(probs, values[:upto])
+            m.of[y, at, window] = m.of[y, at, window] + found.astype(BF)
+
+    for head in range(heads):
+        steps[f"A{head}"] = functools.partial(attend, head)
+
+    own_rows, peer_rows = pl.ds(own_row, count), pl.ds(peer_row, count)
+
+    @step("so")
+    def _():
+        block = m.of.at[y, peer_rows]
+        hop["o"] = send(block, block, m.of.at[oy, own_rows], to_y)
+        block = m.of.at[y, own_rows]
+        hop["o2"] = send(block, block, m.of.at[oy, peer_rows], to_y)
+
+    @step("to")
+    def _():
+        hop["o2"].arrived()
+
+        def transpose_o(index):
+            m.to[pl.ds(index * DEPTH, DEPTH)] = jnp.transpose(m.of[index]).reshape(
+                DEPTH, 2, rows, length
+            )
+
+        loop(2, transpose_o)
+        hop["to"] = send(m.to.at[:, oc], m.tor, m.tor, to_c)
+
+    def mix(index):
+        at = pl.ds(pl.multiple_of(index * half, 128), half)
+        right = weight(3 + index)
+        m.x2[:, at] = m.x[:, at] + (
+            dot_nn(m.of[0, own_rows], right[:half]) + dot_nn(m.of[1, own_rows], right[half:])
+        )
+
+    @step("x2")
+    def _():
+        hop["o"].arrived()
+        ready("o", "O")
+        loop(2, mix)
+
+    def make_h2(index):
+        at = pl.ds(pl.multiple_of(index * STEP_ROWS, STEP_ROWS), STEP_ROWS)
+        values = m.x2[at]
+        normed = values * inverse_rms(values)
+        m.h1[at] = (normed * m.gt[1:2]).astype(BF)
+
+    h2, act = m.h1.at[pl.ds(0, count)], m.h1.at[pl.ds(count, count)]
+
+    @step("h2")
+    def _():
+        hop["h1"].left()
+        loop(count // STEP_ROWS, make_h2)
+
+    @step("th")
+    def _():
+        m.th[...] = jnp.transpose(h2[...]).reshape(2 * DEPTH, 2, rows, count)
+        hop["th"] = send(m.th.at[:, oc], m.thr, m.thr, to_c)
+
+    def back(left, slot, index):
+        at = pl.ds(2 * index, 2)
+        return dot_nt(left[0], m.w[slot, at].reshape(half, half)) + dot_nt(
+            left[1], m.w[slot + 1, at].reshape(half, half)
+        )
+
+    def halves(whole_rows):
+        return whole_rows[:, :half], whole_rows[:, half:]
+
+    def feed(index):
+        at = pl.ds(pl.multiple_of(index * half, 128), half)
+        gate = dot_nn(h2[...], weight(5 + index))
+        m.dh[:, at] = gate
+        act[:, at] = (gate / (1.0 + jnp.exp(-gate))).astype(BF)
+
+    @step("u")
+    def _():
+        ready("up")
+        loop(2, feed)
+
+    @step("tz")
+    def _():
+        m.tz[...] = jnp.transpose(act[...]).reshape(2 * DEPTH, 2, rows, count)
+        hop["tz"] = send(m.tz.at[:, oc], m.tzr, m.tzr, to_c)
+
+    def gate_back(index):
+        at = pl.ds(pl.multiple_of(index * half, 128), half)
+        gate = m.dh[:, at]
+        sigma = 1.0 / (1.0 + jnp.exp(-gate))
+        grad = back(halves(m.gb[0]), 7, index)
+        m.du[0, :, at] = (grad * sigma * (1.0 + gate * (1.0 - sigma))).astype(BF)
+
+    @step("dz")
+    def _():
+        ready("d", "D")
+        loop(2, gate_back)
+        hop["du"] = send(m.du.at[0], m.du.at[1], m.du.at[1], to_c)
+
+    def weight_grad(slot, here, there, rights):
+        def block(index):
+            right_here, right_there = rights()
+            at = pl.ds(DEPTH * index, DEPTH)
+            depth = here.shape[-1]
+            total = dot_nn(here[at, c].reshape(DEPTH * rows, depth), right_here)
+            total = total + dot_nn(there[at].reshape(DEPTH * rows, depth), right_there)
+            m.s[slot, pl.ds(2 * index, 2)] = total.astype(BF).reshape(2, 2, rows, half)
+
+        loop(2, block)
+
+    def column_grad(first, here, there, right):
+        def one(index):
+            at = pl.ds(pl.multiple_of(index * half, 128), half)
+            weight_grad(first + index, here, there, lambda: (right[0, :, at], right[1, :, at]))
+
+        loop(2, one)
+
+    sum_names = ["q", "k", "v", "o", "up", "d0", "d1"]
+    sum_slot = [0, 1, 2, 3, 4 + y, 6, 7]
+    whole = {5: 0, 6: 1}
+    columns = [0, 2, 4, 6, 8, 10, 11]
+
+    def start_x(name):
+        u = sum_names.index(name)
+        for k in (1, 2, 3, 0):
+            target = m.xr.at[u, up_z[k]]
+            hop["sx", u, k] = send(m.s.at[sum_slot[u], up_z[k], ox], target, target, to_x)
+
+    @step("ayup")
+    def _():
+        hop["sy"].arrived()
+        slot = sum_slot[4]
+
+        def block(index):
+            for k in range(2):
+                total = m.s[slot, index, k].astype(F32) + m.yr[index, k].astype(F32)
+                m.s[slot, index, k] = total.astype(BF)
+
+        loop(DEPTH, block)
+        start_x("up")
+
+    def sum_steps(u):
+        name, slot = sum_names[u], sum_slot[u]
+
+        def add_x(k):
+            def body():
+                hop["sx", u, k].arrived()
+                target = up_z[k]
+                total = m.s[slot, target, x].astype(F32) + m.xr[u, target].astype(F32)
+                m.s[slot, target, x] = total.astype(BF)
+                if k:
+                    there = m.zr.at[u, k - 1]
+                    hop["sz", u, k] = send(m.s.at[slot, target, x], there, there, to_z[k])
+
+            return body
+
+        for k in range(DEPTH):
+            steps[f"ax{name}{k}"] = add_x(k)
+
+        @step("az" + name)
+        def _():
+            total = m.s[slot, z, x].astype(F32)
+            for k in range(1, DEPTH):
+                hop["sz", u, k].arrived()
+                total = total + m.zr[u, k - 1].astype(F32)
+            if u in whole:
+                mine, other = m.go.at[whole[u]], m.gr.at[whole[u]]
+                mine[...] = total.astype(BF)
+                hop["se", u] = send(mine, other, other, to_y)
+            else:
+                mine, other = m.g.at[columns[u] + y], m.g.at[columns[u] + oy]
+                mine[...] = total.astype(BF)
+                hop["se", u] = send(mine, mine, other, to_y)
+
+        @step("ae" + name)
+        def _():
+            hop["se", u].arrived()
+            ready_columns = [columns[u]]
+            if u in whole:
+                total = m.go[whole[u]].astype(F32) + m.gr[whole[u]].astype(F32)
+                m.g[columns[u]] = total.astype(BF)
+            else:
+                ready_columns.append(columns[u] + 1)
+            for column in ready_columns:
+                store(m.g.at[column], grad_hbm.at[:, pl.ds(column * half, half)])
+
+    for u in range(len(sum_names)):
+        sum_steps(u)
+
+    stores = []
+
+    def store(source, target):
+        copy = pltpu.make_async_copy(source, target, store_sems.at[len(stores)])
+        copy.start()
+        stores.append(copy)
+
+    @step("Wd")
+    def _():
+        hop["tz"].arrived()
+        hop["gb"].arrived()
+        column_grad(6, m.tz, m.tzr, m.gb)
+        start_x("d0")
+        start_x("d1")
+
+    @step("Wup")
+    def _():
+        hop["th"].arrived()
+        hop["du"].arrived()
+        column_grad(4, m.th, m.thr, m.du)
+        hop["sy"] = send(m.s.at[4 + oy], m.yr, m.yr, to_y)
+
+    @step("Wo")
+    def _():
+        hop["to"].arrived()
+        hop["abc"].arrived()
+        weight_grad(3, m.to, m.tor, lambda: (m.abh[0], m.abh[1]))
+        start_x("o")
+
+    def feed_back(index):
+        at = pl.ds(pl.multiple_of(index * half, 128), half)
+        m.dh[:, at] = back(halves(m.du[0]), 5, index)
+
+    @step("dh2")
+    def _():
+        loop(2, feed_back)
+
+    def norm_back(values, inverse, gain, grad):
+        normed = values * inverse
+        scaled = grad * gain
+        mean = jnp.mean(scaled * normed, axis=-1, keepdims=True)
+        part = jnp.sum((grad * normed).reshape(STEP_ROWS // 8, 8, width), axis=0)
+        return inverse * (scaled - normed * mean), part
+
+    def make_dx2(index):
+        at = pl.ds(pl.multiple_of(index * STEP_ROWS, STEP_ROWS), STEP_ROWS)
+        values = m.x2[at]
+        grad, part = norm_back(values, inverse_rms(values), m.gt[1:2], m.dh[at])
+        m.dg[1] = m.dg[1] + part
+        total = m.cd[at] + grad
+        m.cd[at] = total
+        m.ab[0, at], m.ab[1, at] = halves(total.astype(BF))
+
+    @step("dx2")
+    def _():
+        loop(count // STEP_ROWS, make_dx2)
+
+    @step("do0")
+    def _():
+        m.dos[...] = back((m.ab[0], m.ab[1]), 3, oy).astype(BF)
+        target, arriving = m.dof.at[pl.ds(own_row, count)], m.dof.at[pl.ds(peer_row, count)]
+        hop["do"] = send(m.dos, target, arriving, to_y)
+        m.abh[0, own_rows] = m.ab[y]
+        target, arriving = m.abh.at[0, own_rows], m.abh.at[0, peer_rows]
+        hop["ab"] = send(m.ab.at[oy], target, arriving, to_y)
+
+    @step("abc")
+    def _():
+        hop["ab"].arrived()
+        hop["abc"] = send(m.abh.at[0], m.abh.at[1], m.abh.at[1], to_c)
+
+    @step("do1")
+    def _():
+        m.dof[pl.ds(own_row, count)] = back((m.ab[0], m.ab[1]), 3, y).astype(BF)
+
+    def finish_out(index):
+        at = pl.ds(pl.multiple_of(index * half, 128), half)
+        m.x2[:, at] = m.x2[:, at] + dot_nn(act[...], weight(7 + index))
+
+    @step("out")
+    def _():
+        loop(2, finish_out)
+        store(m.x2, out_hbm)
+
+    def attend_back(head):
+        window, mask = head_window(head)
+        masked_keys = m.qkv[1, :, window] * mask
+        queries = m.qkv[0, :, window] * mask
+        values = m.qkv[2, :, window]
+        grads = m.dof[:, window] * mask
+        key_sum, value_sum = None, None
+        for b in (1, 0):
+            at, upto = slice(b * count, (b + 1) * count), (b + 1) * count
+            low_probs = m.p1[head] if b else m.p0[head]
+            probs = low_probs.astype(F32)
+            grad_probs = dot_nt(values[:upto], grads[at])
+            inner = jnp.sum(probs * grad_probs, axis=0, keepdims=True)
+            low = (probs * (grad_probs - inner)).astype(BF)
+            grad_query = dot_tn(low, masked_keys[:upto])
+            m.dq[0, 0, at, window] = m.dq[0, 0, at, window] + grad_query.astype(BF)
+            value_part = dot_nn(low_probs, grads[at])
+            key_part = dot_nn(low, queries[at])
+            if b:
+                key_sum, value_sum = key_part[:count], value_part[:count]
+                later = slice(count, length)
+                m.dq[0, 1, later, window] = m.dq[0, 1, later, window] + key_part[count:].astype(BF)
+                m.dq[0, 2, later, window] = m.dq[0, 2, later, window] + value_part[count:].astype(BF)
+            else:
+                m.dq[0, 1, at, window] = m.dq[0, 1, at, window] + (key_sum + key_part).astype(BF)
+                m.dq[0, 2, at, window] = m.dq[0, 2, at, window] + (value_sum + value_part).astype(BF)
+
+    def attend_back_step(head):
+        def body():
+            if head == 0:
+                hop["do"].arrived()
+            attend_back(head)
+
+        return body
+
+    for head in range(heads):
+        steps[f"B{head}"] = attend_back_step(head)
+
+    def share(part):
+        hop["d", part] = send(m.dq.at[0, part], m.dq.at[1, part], m.dq.at[1, part], to_c)
+
+    @step("dvk")
+    def _():
+        share(2)
+        share(1)
+
+    def scale_query(index):
+        at = pl.ds(pl.multiple_of(index * STEP_ROWS, STEP_ROWS), STEP_ROWS)
+        values = m.dq[0, 0, at].astype(F32)
+        part = (values * m.qf[at]).reshape(STEP_ROWS // 8, 8, half)
+        m.dg[0, :, :half] = m.dg[0, :, :half] + jnp.sum(part, axis=0)
+        m.dq[0, 0, at] = (values * factor[...]).astype(BF)
+
+    @step("dq")
+    def _():
+        loop(length // STEP_ROWS, scale_query)
+        share(0)
+        m.sm[0] = jnp.zeros_like(m.sm[0])
+        m.sm[0, 2:3] = jnp.sum(m.dg[0], axis=0, keepdims=True)
+        m.dg[0] = jnp.zeros_like(m.dg[0])
+
+    def attention_weight(name):
+        part = "qkv".index(name)
+
+        def body():
+            if name == "v":
+                hop["t1"].arrived()
+            hop["d", part].arrived()
+            weight_grad(part, m.t1, m.t1r, lambda: (m.dq[0, part], m.dq[1, part]))
+            start_x(name)
+
+        return body
+
+    for name in "qkv":
+        steps["W" + name] = attention_weight(name)
+
+    def hidden_back(row, index):
+        at = pl.ds(2 * index, 2)
+        total = None
+        for part in range(3):
+            term = dot_nt(
+                m.dq[0, part, pl.ds(row, count)], m.w[part, at].reshape(half, half)
+            )
+            total = term if total is None else total + term
+        return total
+
+    def hidden_peer(index):
+        at = pl.ds(pl.multiple_of(index * half, 128), half)
+        h2[:, at] = hidden_back(peer_row, index).astype(BF)
+
+    def hidden_own(index):
+        at = pl.ds(pl.multiple_of(index * half, 128), half)
+        m.dh[:, at] = hidden_back(own_row, index)
+
+    @step("dhp")
+    def _():
+        loop(2, hidden_peer)
+        hop["dh"] = send(h2, m.dh1r, m.dh1r, to_y)
+
+    @step("dho")
+    def _():
+        loop(2, hidden_own)
+
+    def make_input_grad(index):
+        at = pl.ds(pl.multiple_of(index * STEP_ROWS, STEP_ROWS), STEP_ROWS)
+        values = m.x[at]
+        grad = m.dh[at] + m.dh1r[at].astype(F32)
+        grad, part = norm_back(values, inverse_rms(values), m.gt[0:1], grad)
+        m.dg[0] = m.dg[0] + part
+        m.cd[at] = m.cd[at] + grad
+
+    @step("ig")
+    def _():
+        hop["dh"].arrived()
+        loop(count // STEP_ROWS, make_input_grad)
+        store(m.cd, grad_in_hbm)
+        for g in range(2):
+            m.sm[0, g:g + 1] = jnp.sum(m.dg[g], axis=0, keepdims=True)
+        hop["smc"] = send(m.sm.at[0], m.smr.at[0], m.smr.at[0], to_c)
+
+    @step("smx")
+    def _():
+        hop["smc"].arrived()
+        m.sm[1] = m.sm[0] + m.smr[0]
+        hop["smx"] = send(m.sm.at[1], m.smr.at[1], m.smr.at[1], to_x)
+
+    @step("smy")
+    def _():
+        hop["smx"].arrived()
+        m.sm[2] = m.sm[1] + m.smr[1]
+        hop["smy"] = send(m.sm.at[2], m.smr.at[2], m.smr.at[2], to_y)
+
+    @step("smz")
+    def _():
+        hop["smy"].arrived()
+        m.smz[z] = m.sm[2] + m.smr[2]
+        block = m.smz.at[z]
+        for k in range(1, DEPTH):
+            hop["smz", k] = send(block, block, m.smz.at[down_z[k]], to_z[k])
+
+    @step("sme")
+    def _():
+        for k in range(1, DEPTH):
+            hop["smz", k].arrived()
+        total = ((m.smz[0] + m.smz[1]) + m.smz[2]) + m.smz[3]
+        m.sm[3] = total
+        m.gs[0:8] = pltpu.roll(total, lax.rem(width - me * rows, width), 1)[:, :128]
+        folded = m.sm[3, 2:3, 0:half]
+        part = folded
+        for head in range(1, heads):
+            part = part + pltpu.roll(folded, half - head * head_dim, 1)
+        m.gs[2:3] = part[:, :128]
+        store(m.gs.at[0:8], small_hbm)
+
+    for name in ORDER:
+        if name == "h1_":
+            hop["h1"].arrived()
+        else:
+            steps[name]()
+    for one in hops:
+        one.left()
+    for copy in stores:
+        copy.wait()
+
+
+def fits(count, groups, owners, width, head_dim, rows):
+    half = width // groups
+    return (
+        groups == 2
+        and owners == 4 * DEPTH
+        and count % 128 == 0
+        and count % STEP_ROWS == 0
+        and rows % 16 == 0
+        and rows == width // owners
+        and half % 128 == 0
+        and half >= 256
+        and half % head_dim == 0
+        and (half // head_dim) % 4 == 0
+        and head_dim <= 128
+    )
+
+
+def fused_layer(
+    inputs,
+    cotangent,
+    starts,
+    weights,
+    weight_m,
+    weight_v,
+    gains,
+    gain_m,
+    gain_v,
+    qscale,
+    qscale_m,
+    qscale_v,
+):
+    count, width = inputs.shape[1:]
+    head_dim = width // HEADS
+    groups = lax.axis_size("seq")
+    half = width // groups
+    rows, columns = weights.shape
+    plan = scratch_plan(count, width, half, rows)
+    anywhere = pl.BlockSpec(memory_space=pl.ANY)
+    inside = pl.BlockSpec(memory_space=pltpu.VMEM)
+    outputs, input_grad, grads, small = pl.pallas_call(
+        functools.partial(layer_kernel, tuple(plan), head_dim),
+        out_shape=(
+            jax.ShapeDtypeStruct((count, width), F32),
+            jax.ShapeDtypeStruct((count, width), F32),
+            jax.ShapeDtypeStruct((rows, columns), BF),
+            jax.ShapeDtypeStruct((8, 128), F32),
+        ),
+        in_specs=[
+            anywhere,
+            anywhere,
+            pl.BlockSpec(memory_space=pltpu.SMEM),
+            anywhere,
+            inside,
+            inside,
+        ],
+        out_specs=(anywhere,) * 4,
+        scratch_shapes=[pltpu.VMEM(shape, kind) for shape, kind in plan.values()]
+        + [
+            pltpu.SemaphoreType.DMA((HOPS,)),
+            pltpu.SemaphoreType.DMA((HOPS,)),
+            pltpu.SemaphoreType.DMA((UNITS + 2,)),
+            pltpu.SemaphoreType.DMA((15,)),
+        ],
+        compiler_params=pltpu.CompilerParams(
+            collective_id=0, has_side_effects=True, vmem_limit_bytes=VMEM_BYTES
+        ),
+    )(inputs[0], cotangent[0], starts, weights, gains, qscale[None])
+    steps = 5
+    block = pl.BlockSpec((rows, columns // steps), lambda index: (0, index))
+    pair = pl.BlockSpec((2, rows), lambda index: (0, 0))
+    single = pl.BlockSpec((1, head_dim), lambda index: (0, 0))
+    tokens = pl.BlockSpec((count, width // steps), lambda index: (0, index))
+    matrix = jax.ShapeDtypeStruct((rows, columns), F32)
+    result = pl.pallas_call(
+        update_kernel,
+        grid=(steps,),
+        out_shape=(outputs, input_grad, matrix, matrix, matrix)
+        + (jax.ShapeDtypeStruct((rows, columns), BF),)
+        + (gains,) * 3
+        + (jax.ShapeDtypeStruct((1, head_dim), F32),) * 3,
+        in_specs=[tokens, tokens, block, pl.BlockSpec((8, 128), lambda index: (0, 0))]
+        + [block] * 3
+        + [pair] * 3
+        + [single] * 3,
+        out_specs=(tokens, tokens) + (block,) * 4 + (pair,) * 3 + (single,) * 3,
+        compiler_params=pltpu.CompilerParams(vmem_limit_bytes=VMEM_BYTES),
+    )(
+        outputs, input_grad, grads, small, weights, weight_m, weight_v, gains, gain_m, gain_v,
+        qscale[None], qscale_m[None], qscale_v[None],
+    )
+    return (result[0][None], result[1][None]) + tuple(result[2:9]) + tuple(
+        value[0] for value in result[9:]
+    )
+
+
+def update_kernel(
+    outputs, input_grad, grads, small, weights, weight_m, weight_v, gains, gain_m, gain_v,
+    qscale, qscale_m, qscale_v, outputs_new, input_grad_new, weights_new, weight_m_new,
+    weight_v_new, weights_low, gains_new, gain_m_new, gain_v_new, qscale_new, qscale_m_new,
+    qscale_v_new
+):
+    outputs_new[...] = outputs[...]
+    input_grad_new[...] = input_grad[...]
+    head_dim = qscale.shape[1]
+
+    @pl.when(pl.program_id(0) == 0)
+    def _():
+        gains_new[...], gain_m_new[...], gain_v_new[...] = adamw(
+            gains[...], small[0:2, : gains.shape[1]], gain_m[...], gain_v[...], RATE_GAIN
+        )
+        slope = QUERY_BASE / math.sqrt(head_dim) / (1.0 + jnp.exp(-qscale[...]))
+        qscale_new[...], qscale_m_new[...], qscale_v_new[...] = adamw(
+            qscale[...], small[2:3, :head_dim] * slope, qscale_m[...], qscale_v[...], RATE_GAIN
+        )
+
+    updated, weight_m_new[...], weight_v_new[...] = adamw(
+        weights[...], grads[...].astype(F32), weight_m[...], weight_v[...], RATE_MATRIX
+    )
+    weights_new[...] = updated
+    weights_low[...] = updated.astype(BF)
+
+
+def on_device(*arrays):
+    count, width = arrays[0].shape[1:]
+    rows = arrays[3].shape[0]
+    if fits(count, lax.axis_size("seq"), lax.axis_size("dp"), width, width // HEADS, rows):
+        return fused_layer(*arrays)
+    return plain_layer(*arrays)
+
+
 def solution(mesh):
     placed = (
         P("dp", "seq", None),
@@ -241,19 +1268,6 @@
         on_device,
         mesh=mesh,
         in_specs=placed,
-        out_specs=(
-            P("dp", "seq", None),
-            P("dp", "seq", None),
-            P("dp", None),
-            P("dp", None),
-            P("dp", None),
-            P("dp", None),
-            P(None, "dp"),
-            P(None, "dp"),
-            P(None, "dp"),
-            P(),
-            P(),
-            P(),
-        ),
+        out_specs=placed[:2] + placed[3:6] + placed[5:],
         check_vma=False,
     )

time: 675 us -> 186 us (0.28); the launches traced: 665 us -> 186 us
  waiting for transfers between devices: 373 us -> 0 us
  Pallas kernels: 0 us -> 185 us
  blocking collectives: 80.5 us -> 0 us
  matrix products: 76.3 us -> 0 us
  local copies, waits for them, and re-layouts: 61.6 us -> 0 us
  other arithmetic: 44.8 us -> 0 us
  starting transfers between devices: 14.2 us -> 0 us
  between operations: 14.7 us -> 0.81 us
    pallas_call x0 -> x2, Pallas kernels: none -> 185 us  [the longest x1 175 us: fused_layer(): pl.pallas_call(functools.partial(layer_kernel, tuple(plan), head_dim), ou...]
    reduce_scatter x1 -> x0, waiting for transfers between devices: 142 us -> none  [on_device(): lax.psum_scatter(all_grads.astype(jnp.bfloat16), 'dp', scatter_dimension=...]
    all_gather x1 -> x0, waiting for transfers between devices: 82 us -> none  [on_device(): lax.all_gather(weights.astype(jnp.bfloat16), 'dp', axis=0, tiled=True)]
    dot_general x18 -> x0, matrix products: 76.3 us -> none  [the longest x1 8.56 us: on_device(): jnp.dot(hidden_one.T, grad_qkv_rows, preferred_element_type=jnp.float32)]
    all_to_all x3 -> x0, waiting for transfers between devices: 57.6 us -> none  [the longest x1 30.9 us: on_device(): lax.all_to_all(outgoing, 'seq', split_axis=2, concat_axis=0, tiled=True)]
    unnamed x5 -> x0, waiting for transfers between devices: 52.9 us -> none
    psum x2 -> x0, blocking collectives: 45.5 us -> none  [the longest x1 40.5 us: on_device(): lax.psum(scale_part, ('dp', 'seq')) * base_scale * jax.nn.sigmoid(qscale)]
    psum x1 -> x0, waiting for transfers between devices: 38.9 us -> none  [on_device(): lax.psum(owned_w.astype(jnp.bfloat16), 'seq').astype(jnp.float32)]
  transfers between devices with their start and end apart: 7 -> 0, of which waited for: 7 -> 0; matrix products, arithmetic and copies ran while one was open for 5% -> 0% of each run, Pallas kernels for 0% -> 0%
where the time goes in v1:
time: 186 us
  Pallas kernels  185 us (99%)
    pallas_call x1, Pallas kernels, fused_layer(): pl.pallas_call(functools.partial(layer_kernel, tuple(plan), head_dim), ou...  175 us
    pallas_call x1, Pallas kernels, fused_layer(): pl.pallas_call(update_kernel, grid=(steps,), out_shape=(outputs, input_gr...  9.81 us

profile of v1, /device:TPU:0, one launch (start us, length us, event | category | flops | bytes accessed | tf_op | source)
XLA Modules:
  0.0 185.7 jit_solution(4103610098677160892)
XLA Ops:
  0.6 175.1 %shard_map.211 = (f32[256,1280]{1,0:T(8,128)}, f32[256,1280]{1,0:T(8,128)}, bf16[80,7680]{1,0:T(8,128)(2,1)}, f32[8,128]{1,0:T(8,128)}) custom-call(f32[256,1280]{1,0:T(8,128)} %bitcast.10, f32[256,1280]{1,0:T(8,128)} %bitcast.11, s32[1,4]{1,0:T(1,128)} %starts.1, f32[80,7680]{1,0:T(8,128)} %weights.1, f32[2,80]{1,0:T(2,128)} %gains.1, f32[1,80]{1,0:T(1,128)} %bitcast.12), custom_call_target="tpu_custom_call" | custom-call | tf_op jit(solution)/shard_map/pallas_call | solution.py:1161
  175.7 9.8 %shard_map.212 = (f32[256,1280]{1,0:T(8,128)}, f32[256,1280]{1,0:T(8,128)}, f32[80,7680]{1,0:T(8,128)}, f32[80,7680]{1,0:T(8,128)}, f32[80,7680]{1,0:T(8,128)}, ...) custom-call(f32[256,1280]{1,0:T(8,128)} %get-tuple-element.28.output, ...), custom_call_target="tpu_custom_call" | custom-call | tf_op jit(solution)/shard_map/pallas_call | solution.py:1195

commit v2 on v1

--- a/solution.py
+++ b/solution.py
@@ -232,7 +232,7 @@
 DEPTH = 4
 STEP_ROWS = 32
 UNITS = 8
-TREE = ("o", "O", "d", "D")
+FIRST_X = ("d", "D")
 VMEM_BYTES = 64 * 1024 * 1024
 
 
@@ -321,7 +321,7 @@
         tor=((2 * DEPTH, rows, length), BF),
         t1=((2 * DEPTH, 2, rows, length), BF),
         t1r=((2 * DEPTH, rows, length), BF),
-        bias=((length, length), F32),
+        bias=((3 * count, count), F32),
         p0=((8, count, count), BF),
         p1=((8, length, count), BF),
         dh1r=((count, width), BF),
@@ -345,20 +345,19 @@
     )
 
 
-HOPS = 168
+HOPS = 176
 ORDER = (
-    "gz", "stv", "stk", "sto", "oxv", "stO", "std", "stq", "gx", "stD", "bias", "stup", "gb",
-    "fzv1", "gc", "fzv2", "h1", "fzv3", "fcv", "oxk", "fzk1", "fxv", "fzk2", "fzk3", "fck", "oxq",
-    "fzq1", "fxk", "fzq2", "h1_", "Pv", "Pk", "fzq3", "oxup", "t1", "fcq", "fzup1", "fxq", "fzup2",
-    "fzup3", "zao", "zaO", "zad", "szD", "Pq", "A0", "fxup", "A1", "zio", "A2", "zaD", "A3", "A4",
-    "ziO", "A5", "A6", "zbo", "A7", "zid", "so", "fcup", "zbO", "fxo", "zbd", "ziD", "fyup", "fxO",
-    "fxd", "x2", "h2", "u", "zbD", "th", "tz", "to", "dz", "dh2", "dx2", "do0", "Wd", "do1", "out",
-    "Wup", "axd01", "axd02", "B0", "axd03", "B1", "B2", "axd11", "abc", "B3", "axd12", "B4",
-    "axd13", "axd10", "Wo", "B5", "B6", "axo1", "B7", "axo2", "dvk", "dq", "axo3", "axd00", "azd0",
-    "ayup", "Wv", "Wk", "axup1", "aed0", "Wq", "axup2", "axo0", "azo", "axup3", "dhp", "dho",
-    "aeo", "axv1", "axup0", "azd1", "axv2", "azup", "axv3", "axv0", "axk1", "axk2", "axk3", "azv",
-    "ig", "axk0", "aed1", "axq1", "smx", "aeup", "axq2", "aev", "axq3", "azk", "axq0", "smy",
-    "aek", "smz", "azq", "sme", "aeq",
+    "gz", "stup", "stD", "stk", "stv", "stq", "stO", "bias", "sto", "std", "gb", "gx", "zaup",
+    "gc", "zav", "ziup", "h1", "ziv", "zbup", "zak", "zbv", "zaq", "zik", "fxup", "h1_", "t1",
+    "ziq", "zbk", "zao", "zbq", "zaO", "szd", "fxv", "zio", "Pv", "ziO", "zad", "szD", "fyup",
+    "zbo", "fxk", "zbO", "zid", "Pk", "zaD", "fxq", "Pq", "A0", "A1", "A2", "A3", "A4", "A5",
+    "ziD", "A6", "A7", "so", "zbd", "fxo", "fxO", "zbD", "x2", "h2", "th", "u", "tz", "dz", "dh2",
+    "dx2", "Wd", "do0", "do1", "out", "to", "axd01", "Wup", "axd02", "axd03", "B0", "B1", "B2",
+    "B3", "B4", "axd11", "B5", "B6", "B7", "dvk", "dq", "axd12", "abc", "axd00", "azd0", "axd13",
+    "Wv", "axd10", "Wk", "Wq", "dhp", "axv1", "dho", "Wo", "azd1", "axv2", "axv3", "axv0", "ayup",
+    "axk1", "aed0", "azv", "axk2", "axk3", "axk0", "axq1", "azk", "axq2", "ig", "axq3", "aed1",
+    "axq0", "smx", "aev", "axo1", "aek", "azq", "axo2", "axo3", "aeq", "axo0", "axup1", "azo",
+    "axup2", "axup3", "aeo", "axup0", "smy", "smz", "azup", "sme", "aeup",
 )
 
 
@@ -390,8 +389,10 @@
     near_z = z + 1 - 2 * lax.rem(z, 2)
     to_near = {"dp": 4 * near_z + 2 * x + c}
     to_middle = {"dp": 4 * (DEPTH - 1 - z) + 2 * x + c}
-    near = pl.ds(2 * lax.div(z, 2), 2)
-    far = pl.ds(2 - 2 * lax.div(z, 2), 2)
+    outer = jnp.logical_not(inner)
+    near_first = 2 * lax.div(z, 2)
+    far_first = 2 - near_first
+    near, far = pl.ds(near_first, 2), pl.ds(far_first, 2)
     hops = []
 
     def send(source, target, arriving, device, when=None, into=None):
@@ -478,17 +479,22 @@
 
     @step("bias")
     def _():
-        position = lax.broadcasted_iota(jnp.int32, (1, length), 1)
-        begin = jnp.zeros((1, length), jnp.int32)
-        for j in range(starts.shape[1]):
-            begin = jnp.maximum(begin, jnp.where(starts[0, j] <= position, starts[0, j], 0))
-
-        def make_bias(index):
-            key = lax.broadcasted_iota(jnp.int32, (STEP_ROWS, length), 0) + index * STEP_ROWS
-            kept = (key <= position) & (key >= begin)
-            m.bias[pl.ds(index * STEP_ROWS, STEP_ROWS)] = jnp.where(kept, 0.0, NEG)
-
-        loop(length // STEP_ROWS, make_bias)
+        def make_bias(first, offset):
+            position = lax.broadcasted_iota(jnp.int32, (1, count), 1) + first
+            begin = jnp.zeros((1, count), jnp.int32)
+            for j in range(starts.shape[1]):
+                begin = jnp.maximum(begin, jnp.where(starts[0, j] <= position, starts[0, j], 0))
+
+            def fill(index):
+                key = lax.broadcasted_iota(jnp.int32, (STEP_ROWS, count), 0) + index * STEP_ROWS
+                kept = (key <= position) & (key >= begin)
+                at = pl.ds(pl.multiple_of(offset + index * STEP_ROWS, STEP_ROWS), STEP_ROWS)
+                m.bias[at] = jnp.where(kept, 0.0, NEG)
+
+            loop((first + count) // STEP_ROWS, fill)
+
+        make_bias(0, 0)
+        make_bias(count, count)
         m.of[y] = jnp.zeros_like(m.of[y])
         m.dq[0] = jnp.zeros_like(m.dq[0])
         m.dg[...] = jnp.zeros_like(m.dg)
@@ -511,52 +517,7 @@
         loop(count // STEP_ROWS, make_h1)
         hop["h1"] = send(h1_own, h1_own, h1_peer, to_y)
 
-    def unit_steps(u):
-        name, slot = names_of[u], unit_slot[u]
-
-        @step("st" + name)
-        def _():
-            loads[u].wait()
-            m.w[slot, z, x, c] = m.wst[u].astype(BF)
-            block = m.w.at[slot, z, x, c]
-            for k in range(1, DEPTH):
-                hop["z", u, k] = send(block, block, m.w.at[slot, down_z[k], x, c], to_z[k])
-
-        def forward(k):
-            def body():
-                if k:
-                    hop["z", u, k].arrived()
-                block = m.w.at[slot, down_z[k], x, c]
-                hop["x", u, k] = send(block, block, m.w.at[slot, down_z[k], ox, c], to_x)
-
-            return body
-
-        steps["ox" + name] = forward(0)
-        for k in range(1, DEPTH):
-            steps[f"fz{name}{k}"] = forward(k)
-
-        @step("fc" + name)
-        def _():
-            block = m.w.at[slot, :, x, c]
-            hop["c", u, 0] = send(block, block, m.w.at[slot, :, x, oc], to_c)
-
-        @step("fx" + name)
-        def _():
-            for k in range(DEPTH):
-                hop["x", u, k].arrived()
-            if name == "up":
-                block = m.w.at[slot, :, :, c]
-                hop["y", u] = send(block, block, m.w.at[swap_slot, :, :, c], to_y)
-            block = m.w.at[slot, :, ox, c]
-            hop["c", u, 1] = send(block, block, m.w.at[slot, :, ox, oc], to_c)
-
-        @step("fy" + name)
-        def _():
-            hop["y", u].arrived()
-            block = m.w.at[swap_slot, :, :, c]
-            hop["yc", u] = send(block, block, m.w.at[swap_slot, :, :, oc], to_c)
-
-    def tree_steps(u, first_x):
+    def unit_steps(u, first_x):
         name, slot = names_of[u], unit_slot[u]
         side = slice(None) if first_x else x
 
@@ -599,7 +560,7 @@
 
         @step("zb" + name)
         def _():
-            pl.when(jnp.logical_not(inner))(hop["zb", u].arrived)
+            pl.when(outer)(hop["zb", u].arrived)
             if first_x:
                 block = m.w.at[slot, :, :, c]
                 hop["c", u, 1] = send(block, block, m.w.at[slot, :, :, oc], to_c)
@@ -613,14 +574,20 @@
         def _():
             hop["xa", u].arrived()
             hop["xb", u].arrived()
+            if name == "up":
+                block = m.w.at[slot, :, :, c]
+                hop["y", u] = send(block, block, m.w.at[swap_slot, :, :, c], to_y)
             block = m.w.at[slot, :, ox, c]
             hop["c", u, 1] = send(block, block, m.w.at[slot, :, ox, oc], to_c)
 
+        @step("fy" + name)
+        def _():
+            hop["y", u].arrived()
+            block = m.w.at[swap_slot, :, :, c]
+            hop["yc", u] = send(block, block, m.w.at[swap_slot, :, :, oc], to_c)
+
     for u in range(UNITS):
-        if names_of[u] in TREE:
-            tree_steps(u, names_of[u] == TREE[-1])
-        else:
-            unit_steps(u)
+        unit_steps(u, names_of[u] in FIRST_X)
 
     def ready(*wanted):
         for name in wanted:
@@ -677,7 +644,8 @@
         values = m.qkv[2, :, window] * mask
         for b in range(2):
             at, upto = slice(b * count, (b + 1) * count), (b + 1) * count
-            scores = dot_nt(keys[:upto], queries[at]) + m.bias[:upto, at]
+            allowed = m.bias[pl.ds(b * count, upto)]
+            scores = dot_nt(keys[:upto], queries[at]) + allowed
             top = jnp.max(scores, axis=0, keepdims=True)
             expo = jnp.exp(scores - top)
             total = jnp.sum(expo, axis=0, keepdims=True)

time: 186 us -> 183 us (0.984)
  Pallas kernels: 185 us -> 182 us
    pallas_call x1, Pallas kernels: 175 us -> 172 us  [fused_layer(): pl.pallas_call(functools.partial(layer_kernel, tuple(plan), head_dim), ou...]
where the time goes in v2:
time: 183 us
  Pallas kernels  182 us (99%)
    pallas_call x1, Pallas kernels, fused_layer(): pl.pallas_call(functools.partial(layer_kernel, tuple(plan), head_dim), ou...  172 us
    pallas_call x1, Pallas kernels, fused_layer(): pl.pallas_call(update_kernel, grid=(steps,), out_shape=(outputs, input_gr...  9.81 us

profile of v2, /device:TPU:0, one launch (start us, length us, event | category | flops | bytes accessed | tf_op | source)
XLA Modules:
  0.0 182.9 jit_solution(13980682416390896223)
XLA Ops:
  0.6 172.3 %shard_map.211 = (f32[256,1280]{1,0:T(8,128)}, f32[256,1280]{1,0:T(8,128)}, bf16[80,7680]{1,0:T(8,128)(2,1)}, f32[8,128]{1,0:T(8,128)}) custom-call(f32[256,1280]{1,0:T(8,128)} %bitcast.10, f32[256,1280]{1,0:T(8,128)} %bitcast.11, s32[1,4]{1,0:T(1,128)} %starts.1, f32[80,7680]{1,0:T(8,128)} %weights.1, f32[2,80]{1,0:T(2,128)} %gains.1, f32[1,80]{1,0:T(1,128)} %bitcast.12), custom_call_target="tpu_custom_call" | custom-call | tf_op jit(solution)/shard_map/pallas_call | solution.py:1129
  172.9 9.8 %shard_map.212 = (f32[256,1280]{1,0:T(8,128)}, f32[256,1280]{1,0:T(8,128)}, f32[80,7680]{1,0:T(8,128)}, f32[80,7680]{1,0:T(8,128)}, f32[80,7680]{1,0:T(8,128)}, ...) custom-call(f32[256,1280]{1,0:T(8,128)} %get-tuple-element.28.output, ...), custom_call_target="tpu_custom_call" | custom-call | tf_op jit(solution)/shard_map/pallas_call | solution.py:1163

commit v3 on v2

--- a/solution.py
+++ b/solution.py
@@ -347,16 +347,16 @@
 
 HOPS = 176
 ORDER = (
-    "gz", "stup", "stD", "stk", "stv", "stq", "stO", "bias", "sto", "std", "gb", "gx", "zaup",
-    "gc", "zav", "ziup", "h1", "ziv", "zbup", "zak", "zbv", "zaq", "zik", "fxup", "h1_", "t1",
-    "ziq", "zbk", "zao", "zbq", "zaO", "szd", "fxv", "zio", "Pv", "ziO", "zad", "szD", "fyup",
-    "zbo", "fxk", "zbO", "zid", "Pk", "zaD", "fxq", "Pq", "A0", "A1", "A2", "A3", "A4", "A5",
-    "ziD", "A6", "A7", "so", "zbd", "fxo", "fxO", "zbD", "x2", "h2", "th", "u", "tz", "dz", "dh2",
-    "dx2", "Wd", "do0", "do1", "out", "to", "axd01", "Wup", "axd02", "axd03", "B0", "B1", "B2",
-    "B3", "B4", "axd11", "B5", "B6", "B7", "dvk", "dq", "axd12", "abc", "axd00", "azd0", "axd13",
-    "Wv", "axd10", "Wk", "Wq", "dhp", "axv1", "dho", "Wo", "azd1", "axv2", "axv3", "axv0", "ayup",
-    "axk1", "aed0", "azv", "axk2", "axk3", "axk0", "axq1", "azk", "axq2", "ig", "axq3", "aed1",
-    "axq0", "smx", "aev", "axo1", "aek", "azq", "axo2", "axo3", "aeq", "axo0", "axup1", "azo",
+    "gz", "stup", "stD", "stv", "stO", "std", "stk", "sto", "bias", "stq", "gx", "gb", "zav",
+    "zaup", "gc", "h1", "zak", "ziv", "zaq", "ziup", "zbv", "zao", "zik", "zbup", "zaO", "szd",
+    "ziq", "h1_", "t1", "zbk", "zio", "fxv", "zad", "szD", "ziO", "Pv", "zbq", "zbo", "fxup",
+    "zid", "zaD", "zbO", "fxk", "Pk", "ziD", "fxq", "zbd", "Pq", "A0", "A1", "A2", "A3", "A4",
+    "A5", "A6", "A7", "so", "fxo", "fyup", "fxO", "zbD", "x2", "h2", "u", "tz", "dz", "dh2", "dx2",
+    "do0", "Wd", "do1", "to", "out", "axd01", "th", "axd02", "B0", "B1", "axd03", "B2", "B3",
+    "axd00", "B4", "B5", "axd11", "B6", "B7", "azd0", "axd12", "dvk", "dq", "Wup", "axd13", "abc",
+    "Wv", "Wk", "Wq", "dhp", "axv1", "Wo", "aed0", "axd10", "azd1", "axv2", "dho", "axv3", "axv0",
+    "axk1", "azv", "axk2", "ayup", "axk3", "axk0", "axq1", "azk", "axq2", "axq3", "axq0", "ig",
+    "axo1", "aed1", "smx", "azq", "axo2", "aev", "aek", "axo3", "aeq", "axo0", "axup1", "azo",
     "axup2", "axup3", "aeo", "axup0", "smy", "smz", "azup", "sme", "aeup",
 )
 

time: 183 us -> 182 us (level)
  no operation moved by 1% of the time
where the time goes in v3:
time: 182 us; the launch traced here: 181 us
  Pallas kernels  181 us (99%)
    pallas_call x1, Pallas kernels, fused_layer(): pl.pallas_call(functools.partial(layer_kernel, tuple(plan), head_dim), ou...  171 us
    pallas_call x1, Pallas kernels, fused_layer(): pl.pallas_call(update_kernel, grid=(steps,), out_shape=(outputs, input_gr...  9.81 us

profile of v3, /device:TPU:0, one launch (start us, length us, event | category | flops | bytes accessed | tf_op | source)
XLA Modules:
  0.0 181.4 jit_solution(9737634163233584702)
XLA Ops:
  0.6 170.8 %shard_map.211 = (f32[256,1280]{1,0:T(8,128)}, f32[256,1280]{1,0:T(8,128)}, bf16[80,7680]{1,0:T(8,128)(2,1)}, f32[8,128]{1,0:T(8,128)}) custom-call(f32[256,1280]{1,0:T(8,128)} %bitcast.10, f32[256,1280]{1,0:T(8,128)} %bitcast.11, s32[1,4]{1,0:T(1,128)} %starts.1, f32[80,7680]{1,0:T(8,128)} %weights.1, f32[2,80]{1,0:T(2,128)} %gains.1, f32[1,80]{1,0:T(1,128)} %bitcast.12), custom_call_target="tpu_custom_call" | custom-call | tf_op jit(solution)/shard_map/pallas_call | solution.py:1129
  171.4 9.8 %shard_map.212 = (f32[256,1280]{1,0:T(8,128)}, f32[256,1280]{1,0:T(8,128)}, f32[80,7680]{1,0:T(8,128)}, f32[80,7680]{1,0:T(8,128)}, f32[80,7680]{1,0:T(8,128)}, ...) custom-call(f32[256,1280]{1,0:T(8,128)} %get-tuple-element.28.output, ...), custom_call_target="tpu_custom_call" | custom-call | tf_op jit(solution)/shard_map/pallas_call | solution.py:1163
